TPU v7x, 256 devices: a whole 4x4x8 slice. The times are simulated.
256 devices in a mesh: rows: 64 (over z, x, core), sub: 4 (over y).
Axes of the slice: x: 4, y: 4, z: 8, core: 2. Of those that a mesh axis runs over, the one named last changes fastest.
Arguments:
- embeddings: float32 [131072, 256], P('rows'), may hold values from -6 to 6
- start_vectors: float32 [131072, 64], P('rows'), may hold values from -6 to 6
- pairs: int32 [512, 2], P('rows'), may hold values from -1 to 127, as said below
Outputs:
- vectors: float32 [131072, 64], P('rows')
Inputs may be any that keep to these rules, and one draw needn't show every extreme that they name: Slot s of row group g is entry g * 8 + s. A group's pairs have row block 2g or 2g+1 (owned by the group) and column block j with row block <= j <= 2g+3 and j < 128; no pair is listed twice; both diagonal pairs (2g, 2g) and (2g+1, 2g+1) are listed; used slots come first, empty slots hold -1 in both entries; at most 7 slots of a group are used and group 0 uses 7.
All inputs are finite; a program needn't handle non-finite values.
Results may differ from a plain program's by a relative error of at most 0.0003.
Values sent between devices are 32-bit elements; how exact they have to be, the bound alone decides.
No kernel may reach another device: no remote copies, remote signals or barrier semaphores. Data moves between devices by JAX's collectives and lax.ppermute only.
A program may use at most 64 MiB of HBM per device.

v0:
```python
import jax
import jax.numpy as jnp
from jax import lax
from jax.sharding import PartitionSpec as P

BLK_DEV = 2
ITERS = 2
inverse_width = 1.0 / 64.0
highest = lax.Precision.HIGHEST


def shifted(array, axis, by):
    devices = lax.axis_size(axis)
    pairs = [(i, i + by) for i in range(devices) if 0 <= i + by < devices]
    return lax.ppermute(array, axis, pairs)


def tile_terms(ext_embed, ext_norms, ext_vec, mine, first_block, block, row_count):

    def visit(slot, acc):
        row_block = mine[slot, 0]
        col_block = mine[slot, 1]

        def work(inner):
            row_start = (row_block - first_block) * block
            col_start = (col_block - first_block) * block
            xa = lax.dynamic_slice_in_dim(ext_embed, row_start, row_count, 0)
            xb = lax.dynamic_slice_in_dim(ext_embed, col_start, block, 0)
            na = lax.dynamic_slice_in_dim(ext_norms, row_start, row_count, 0)
            nb = lax.dynamic_slice_in_dim(ext_norms, col_start, block, 0)
            dots = lax.dot_general(
                xa,
                xb,
                (((1,), (1,)), ((), ())),
                precision=highest,
                preferred_element_type=jnp.float32,
            )
            dist = jnp.maximum(na[:, None] + nb[None, :] - 2.0 * dots, 0.0)
            affinity = jnp.exp(-dist * inverse_width)
            va = lax.dynamic_slice_in_dim(ext_vec, row_start, row_count, 0)
            vb = lax.dynamic_slice_in_dim(ext_vec, col_start, block, 0)
            ahead = jnp.dot(affinity, vb, precision=highest, preferred_element_type=jnp.float32)
            behind = lax.dot_general(
                affinity,
                va,
                (((0,), (0,)), ((), ())),
                precision=highest,
                preferred_element_type=jnp.float32,
            )
            behind = behind * (row_block != col_block).astype(jnp.float32)
            current = lax.dynamic_slice_in_dim(inner, row_start, row_count, 0)
            inner = lax.dynamic_update_slice_in_dim(inner, current + ahead, row_start, 0)
            current = lax.dynamic_slice_in_dim(inner, col_start, block, 0)
            return lax.dynamic_update_slice_in_dim(inner, current + behind, col_start, 0)

        return lax.cond(row_block >= 0, work, lambda inner: inner, acc)

    start_acc = jnp.zeros(ext_vec.shape, jnp.float32)
    return lax.fori_loop(0, mine.shape[0], visit, start_acc)


def gram_of(share, total_rows):
    return (
        lax.dot_general(
            share,
            share,
            (((0,), (0,)), ((), ())),
            precision=highest,
            preferred_element_type=jnp.float32,
        )
        / total_rows
    )


def right_solve(lower, image):
    return lax.linalg.triangular_solve(lower, image, left_side=False, lower=True, transpose_a=True)


def on_device(embeddings, start_vectors, pairs):
    group = lax.axis_index("rows")
    member = lax.axis_index("sub")
    members = lax.axis_size("sub")
    rows_own = embeddings.shape[0]
    block = rows_own // BLK_DEV
    quarter = rows_own // members
    total_rows = rows_own * lax.axis_size("rows")
    first_block = group * BLK_DEV
    per_member = pairs.shape[0] // members
    slot_ids = member * per_member + jnp.arange(per_member, dtype=jnp.int32)
    mine = jnp.take(pairs, slot_ids, axis=0)
    next_embed, next_vec = shifted((embeddings, start_vectors), "rows", -1)
    ext_embed = jnp.concatenate([embeddings, next_embed], axis=0)
    ext_norms = jnp.sum(ext_embed * ext_embed, axis=1)
    own_vec = start_vectors
    whole = start_vectors
    share = start_vectors[:quarter]
    for step in range(ITERS):
        ext_vec = jnp.concatenate([own_vec, next_vec], axis=0)
        terms = tile_terms(ext_embed, ext_norms, ext_vec, mine, first_block, block, block)
        own_part = terms[:rows_own]
        spill_part = terms[rows_own:]
        own_sum, spill_sum = lax.psum((own_part, spill_part), "sub")
        incoming = shifted(spill_sum, "rows", 1)
        whole = own_sum + incoming
        share = lax.dynamic_slice_in_dim(whole, member * quarter, quarter, 0)
        gram_part = gram_of(share, total_rows)
        gram = lax.psum(gram_part, ("rows", "sub"))
        lower = jnp.linalg.cholesky(gram)
        whole = right_solve(lower, whole)
        if step + 1 < ITERS:
            own_vec = whole
            next_vec = shifted(whole, "rows", -1)
    return whole


def solution(mesh):
    return jax.shard_map(
        on_device,
        mesh=mesh,
        in_specs=(P("rows", None), P("rows", None), P("rows", None)),
        out_specs=P("rows", None),
        check_vma=False,
    )
```

profile of v0, /device:TPU:1, one launch (start us, length us, event | category | flops | bytes accessed | tf_op | source)
XLA Modules:
  0.0 469.9 jit_solution(7890683646325873900)
XLA Ops:
  6.5 5.3 %collective-permute-start = (f32[2048,256]{1,0:T(8,128)}, f32[2048,256]{1,0:T(8,128)}, u32[]{:S(2)}, u32[]{:S(2)}) collective-permute-start(f32[2048,256]{1,0:T(8,128)} %param.14), channel_id=1, source_target_pairs={{4,0},{8,4},{12,8},{16,12},{20,16},{24,20},{28,24},{32,28},{36,32}... | collective-permute-start | bytes 6291464 | tf_op jit(solution)/shard_map/ppermute | solution.py:15
  11.8 1.9 collective-permute-start.1
  13.8 0.8 copy.12
  15.2 3.1 constant_dynamic-update-slice_fusion.1
  18.2 22.5 %collective-permute-done.1 = f32[2048,64]{0,1:T(8,128)S(1)} collective-permute-done((f32[2048,64]{0,1:T(8,128)}, f32[2048,64]{0,1:T(8,128)S(1)}, u32[]{:S(2)}, u32[]{:S(2)}) %collective-permute-start.1) | collective-permute-done | bytes 524320 | tf_op jit(solution)/shard_map/ppermute | solution.py:15
  41.4 3.0 constant_dynamic-update-slice_fusion
  44.4 2.8 multiply_reduce_fusion
  47.3 46.1 %while.32 = (s32[]{:T(128)}, f32[4096,64]{0,1:T(8,128)S(1)}, s32[2,2]{1,0:T(2,128)S(1)}, s32[]{:T(128)}, f32[4096]{0:T(1024)S(1)}, /*index=5*/f32[4096,256]{1,0:...) while((s32[]{:T(128)}, f32[4096,64]{0,1:T(8,128)S(1)}, s32[2,2]{1,0:T(2,128)S(1)}, s32[]{:T(128)}, ...), condition=%wide.region_4.5_spmd, body=%wide.region_1.0_spmd.sunk | while | flops 4844617728 | bytes 33587592 | solution.py:59
  48.5 21.9 %conditional.4 = (f32[4096,64]{0,1:T(8,128)S(1)}) conditional(s32[]{:T(128)} %convert_element_type.22, f32[4096,64]{0,1:T(8,128)S(1)} %get-tuple-element.484, (s32[]{:T(128)}, s32[]{:T(128)}, f32[4096,64]{0,1:T(8,128)S(1)}, f32[4096]{0:T(1024)S(1)}, s32[2,2]{1,0:T(2,128)S(1)}, /*index=5*/s32[]{:T(128)}, f32[4096,256]{1,0:T(8,128)}, ...), branch_computations={%region_2.2_spmd, %region_3.3_spmd} | conditional | flops 4844617728 | bytes 33587412 | solution.py:56
  50.5 5.3 %fusion.17 = f32[1024,1024]{1,0:T(8,128)S(1)} fusion(f32[4096,256]{1,0:T(8,128)} %get-tuple-element.297, s32[]{:T(128)S(6)} %select_n.59, s32[]{:T(128)S(6)} %select_n.58), kind=kOutput, calls=%fused_computation.19 | convolution fusion | flops 3221225472 | bytes 6291464 | tf_op jit(solution)/shard_map/while/body/eval_jaxpr/cond/branch_1_fun/dot_general | solution.py:31
  55.8 2.0 copy-done
  57.8 5.3 %fusion.13 = f32[4096,64]{0,1:T(8,128)S(1)} fusion(f32[4096,64]{0,1:T(8,128)S(1)} %get-tuple-element.291, s32[]{:T(128)S(6)} %select_n.58, f32[1024,1024]{1,0:T(8,128)S(1)} %fusion.17, f32[1024]{0:T(1024)S(1)} %get-tuple-element.381, f32[1024]{0:T(1024)S(1)} %get-tuple-element.380, f32[4096,64]{1,0:T(8,128)S(1)} %get-tuple-element.298, s32[]{:T(128)S(6)} %select_n.59), kind=kOutput, calls=%fused_computation.15 | convolution fusion | flops 811663360 | bytes 5251080 | tf_op jit(solution)/shard_map/while/body/eval_jaxpr/cond/branch_1_fun/dot_general | solution.py:42
  64.3 6.0 %fusion.16 = f32[4096,64]{0,1:T(8,128)S(1)} fusion(f32[4096,64]{0,1:T(8,128)S(1)} %fusion.13, s32[]{:T(128)S(6)} %select_n.59, f32[1024,1024]{1,0:T(8,128)} %copy-done, f32[1024]{0:T(1024)S(1)} %get-tuple-element.381, f32[1024]{0:T(1024)S(1)} %get-tuple-element.380, f32[4096,64]{1,0:T(8,128)S(1)} %get-tuple-element.298, s32[]{:T(128)S(6)} %select_n.58, ...), kind=kOutput, calls=%fused_computation.18 | convolution fusion | flops 811728896 | bytes 5251084 | tf_op jit(solution)/shard_map/while/body/eval_jaxpr/cond/branch_1_fun/dot_general | solution.py:43
  71.6 21.9 %conditional.4 = (f32[4096,64]{0,1:T(8,128)S(1)}) conditional(s32[]{:T(128)} %convert_element_type.22, f32[4096,64]{0,1:T(8,128)S(1)} %get-tuple-element.484, (s32[]{:T(128)}, s32[]{:T(128)}, f32[4096,64]{0,1:T(8,128)S(1)}, f32[4096]{0:T(1024)S(1)}, s32[2,2]{1,0:T(2,128)S(1)}, /*index=5*/s32[]{:T(128)}, f32[4096,256]{1,0:T(8,128)}, ...), branch_computations={%region_2.2_spmd, %region_3.3_spmd} | conditional | flops 4844617728 | bytes 33587412 | solution.py:56
  73.6 5.3 %fusion.17 = f32[1024,1024]{1,0:T(8,128)S(1)} fusion(f32[4096,256]{1,0:T(8,128)} %get-tuple-element.297, s32[]{:T(128)S(6)} %select_n.59, s32[]{:T(128)S(6)} %select_n.58), kind=kOutput, calls=%fused_computation.19 | convolution fusion | flops 3221225472 | bytes 6291464 | tf_op jit(solution)/shard_map/while/body/eval_jaxpr/cond/branch_1_fun/dot_general | solution.py:31
  78.9 2.0 copy-done
  80.8 5.3 %fusion.13 = f32[4096,64]{0,1:T(8,128)S(1)} fusion(f32[4096,64]{0,1:T(8,128)S(1)} %get-tuple-element.291, s32[]{:T(128)S(6)} %select_n.58, f32[1024,1024]{1,0:T(8,128)S(1)} %fusion.17, f32[1024]{0:T(1024)S(1)} %get-tuple-element.381, f32[1024]{0:T(1024)S(1)} %get-tuple-element.380, f32[4096,64]{1,0:T(8,128)S(1)} %get-tuple-element.298, s32[]{:T(128)S(6)} %select_n.59), kind=kOutput, calls=%fused_computation.15 | convolution fusion | flops 811663360 | bytes 5251080 | tf_op jit(solution)/shard_map/while/body/eval_jaxpr/cond/branch_1_fun/dot_general | solution.py:42
  87.4 6.0 %fusion.16 = f32[4096,64]{0,1:T(8,128)S(1)} fusion(f32[4096,64]{0,1:T(8,128)S(1)} %fusion.13, s32[]{:T(128)S(6)} %select_n.59, f32[1024,1024]{1,0:T(8,128)} %copy-done, f32[1024]{0:T(1024)S(1)} %get-tuple-element.381, f32[1024]{0:T(1024)S(1)} %get-tuple-element.380, f32[4096,64]{1,0:T(8,128)S(1)} %get-tuple-element.298, s32[]{:T(128)S(6)} %select_n.58, ...), kind=kOutput, calls=%fused_computation.18 | convolution fusion | flops 811728896 | bytes 5251084 | tf_op jit(solution)/shard_map/while/body/eval_jaxpr/cond/branch_1_fun/dot_general | solution.py:43
  93.4 1.1 fusion.78
  94.6 53.3 %all-reduce.7.cloned.1.call-done = (f32[2048,64]{0,1:T(8,128)}, f32[2048,64]{0,1:T(8,128)}) async-done(((f32[2048,64]{0,1:T(8,128)}, f32[2048,64]{0,1:T(8,128)}), (f32[2048,64]{0,1:T(8,128)}, f32[2048,64]{0,1:T(8,128)})) %all-reduce.7.cloned.1.call-update) | async-done | bytes 1048592 | tf_op jit(solution)/shard_map/psum | solution.py:102
  147.9 5.0 %collective-permute-start.2 = (f32[2048,64]{0,1:T(8,128)}, f32[2048,64]{0,1:T(8,128)S(1)}, u32[]{:S(2)}, u32[]{:S(2)}) collective-permute-start(f32[2048,64]{0,1:T(8,128)} %get-tuple-element.379), channel_id=1, source_target_pairs={{0,4},{4,8},{8,12},{12,16},{16,20},{20,24},{24,28},{28,32},{32,36}... | collective-permute-start | bytes 1572872 | tf_op jit(solution)/shard_map/ppermute | solution.py:15
  152.9 6.4 %collective-permute-done.2 = f32[2048,64]{0,1:T(8,128)S(1)} collective-permute-done((f32[2048,64]{0,1:T(8,128)}, f32[2048,64]{0,1:T(8,128)S(1)}, u32[]{:S(2)}, u32[]{:S(2)}) %collective-permute-start.2) | collective-permute-done | bytes 524320 | tf_op jit(solution)/shard_map/ppermute | solution.py:15
  159.3 1.1 add.180
  160.7 78.2 %psum.44 = f32[64,64]{0,1:T(8,128)S(1)} all-reduce(f32[64,64]{0,1:T(8,128)S(1)} %convolution_multiply_fusion.1), channel_id=1, replica_groups=mesh['rows'=64,'sub'=4] {'rows','sub'}, use_global_device_ids=true, to_apply=%region_7.8 | all-reduce | flops 4096 | bytes 32768 | tf_op jit(solution)/shard_map/psum | solution.py:107
  238.9 5.8 %cholesky.44 = f32[64,64]{1,0:T(8,128)S(1)} custom-call(f32[64,64]{1,0:T(8,128)S(1)} %fusion.69), custom_call_target="Cholesky" | custom-call | tf_op jit(solution)/shard_map/jit(cholesky)/cholesky | solution.py:108
  246.1 4.9 %custom-call.6 = f32[1,64,64]{1,2,0:T(8,128)S(1)} custom-call(f32[1,64,64]{2,1,0:T(8,128)S(1)} %fusion.64), custom_call_target="InvertDiagBlocksLowerTriangular" | custom-call | tf_op jit(solution)/shard_map/triangular_solve/custom-call.0 | solution.py:76
  251.7 2.9 collective-permute-start.3
  254.5 7.6 %collective-permute-done.3 = f32[2048,64]{0,1:T(8,128)S(1)} collective-permute-done((f32[2048,64]{0,1:T(8,128)S(1)}, f32[2048,64]{0,1:T(8,128)S(1)}, u32[]{:S(2)}, u32[]{:S(2)}) %collective-permute-start.3) | collective-permute-done | bytes 524320 | tf_op jit(solution)/shard_map/ppermute | solution.py:15
  262.9 46.1 %while.33 = (s32[]{:T(128)}, f32[4096,64]{0,1:T(8,128)S(1)}, s32[2,2]{1,0:T(2,128)S(1)}, s32[]{:T(128)}, f32[4096]{0:T(1024)S(1)}, /*index=5*/f32[4096,256]{1,0:...) while((s32[]{:T(128)}, f32[4096,64]{0,1:T(8,128)S(1)}, s32[2,2]{1,0:T(2,128)S(1)}, s32[]{:T(128)}, ...), condition=%wide.region_13.16_spmd, body=%wide.region_10.15_spmd.sunk | while | flops 4844617728 | bytes 33587592 | solution.py:59
  264.1 21.9 %conditional.5 = (f32[4096,64]{0,1:T(8,128)S(1)}) conditional(s32[]{:T(128)} %convert_element_type.23, f32[4096,64]{0,1:T(8,128)S(1)} %get-tuple-element.511, (s32[]{:T(128)}, s32[]{:T(128)}, f32[4096,64]{0,1:T(8,128)S(1)}, f32[4096]{0:T(1024)S(1)}, s32[2,2]{1,0:T(2,128)S(1)}, /*index=5*/s32[]{:T(128)}, f32[4096,256]{1,0:T(8,128)}, ...), branch_computations={%region_11.13_spmd, %region_12.14_spmd} | conditional | flops 4844617728 | bytes 33587412 | solution.py:56
  266.1 5.3 %fusion.48 = f32[1024,1024]{1,0:T(8,128)S(1)} fusion(f32[4096,256]{1,0:T(8,128)} %get-tuple-element.313, s32[]{:T(128)S(6)} %select_n.62, s32[]{:T(128)S(6)} %select_n.61), kind=kOutput, calls=%fused_computation.53 | convolution fusion | flops 3221225472 | bytes 6291464 | tf_op jit(solution)/shard_map/while/body/eval_jaxpr/cond/branch_1_fun/dot_general | solution.py:31
  271.4 2.0 copy-done.1
  273.4 5.3 %fusion.44 = f32[4096,64]{0,1:T(8,128)S(1)} fusion(f32[4096,64]{0,1:T(8,128)S(1)} %get-tuple-element.307, s32[]{:T(128)S(6)} %select_n.61, f32[1024,1024]{1,0:T(8,128)S(1)} %fusion.48, f32[1024]{0:T(1024)S(1)} %get-tuple-element.383, f32[1024]{0:T(1024)S(1)} %get-tuple-element.382, f32[4096,64]{1,0:T(8,128)S(1)} %get-tuple-element.314, s32[]{:T(128)S(6)} %select_n.62), kind=kOutput, calls=%fused_computation.49 | convolution fusion | flops 811663360 | bytes 5251080 | tf_op jit(solution)/shard_map/while/body/eval_jaxpr/cond/branch_1_fun/dot_general | solution.py:42
  279.9 6.0 %fusion.47 = f32[4096,64]{0,1:T(8,128)S(1)} fusion(f32[4096,64]{0,1:T(8,128)S(1)} %fusion.44, s32[]{:T(128)S(6)} %select_n.62, f32[1024,1024]{1,0:T(8,128)} %copy-done.1, f32[1024]{0:T(1024)S(1)} %get-tuple-element.383, f32[1024]{0:T(1024)S(1)} %get-tuple-element.382, f32[4096,64]{1,0:T(8,128)S(1)} %get-tuple-element.314, s32[]{:T(128)S(6)} %select_n.61, ...), kind=kOutput, calls=%fused_computation.52 | convolution fusion | flops 811728896 | bytes 5251084 | tf_op jit(solution)/shard_map/while/body/eval_jaxpr/cond/branch_1_fun/dot_general | solution.py:43
  287.1 21.9 %conditional.5 = (f32[4096,64]{0,1:T(8,128)S(1)}) conditional(s32[]{:T(128)} %convert_element_type.23, f32[4096,64]{0,1:T(8,128)S(1)} %get-tuple-element.511, (s32[]{:T(128)}, s32[]{:T(128)}, f32[4096,64]{0,1:T(8,128)S(1)}, f32[4096]{0:T(1024)S(1)}, s32[2,2]{1,0:T(2,128)S(1)}, /*index=5*/s32[]{:T(128)}, f32[4096,256]{1,0:T(8,128)}, ...), branch_computations={%region_11.13_spmd, %region_12.14_spmd} | conditional | flops 4844617728 | bytes 33587412 | solution.py:56
  289.1 5.3 %fusion.48 = f32[1024,1024]{1,0:T(8,128)S(1)} fusion(f32[4096,256]{1,0:T(8,128)} %get-tuple-element.313, s32[]{:T(128)S(6)} %select_n.62, s32[]{:T(128)S(6)} %select_n.61), kind=kOutput, calls=%fused_computation.53 | convolution fusion | flops 3221225472 | bytes 6291464 | tf_op jit(solution)/shard_map/while/body/eval_jaxpr/cond/branch_1_fun/dot_general | solution.py:31
  294.5 2.0 copy-done.1
  296.4 5.3 %fusion.44 = f32[4096,64]{0,1:T(8,128)S(1)} fusion(f32[4096,64]{0,1:T(8,128)S(1)} %get-tuple-element.307, s32[]{:T(128)S(6)} %select_n.61, f32[1024,1024]{1,0:T(8,128)S(1)} %fusion.48, f32[1024]{0:T(1024)S(1)} %get-tuple-element.383, f32[1024]{0:T(1024)S(1)} %get-tuple-element.382, f32[4096,64]{1,0:T(8,128)S(1)} %get-tuple-element.314, s32[]{:T(128)S(6)} %select_n.62), kind=kOutput, calls=%fused_computation.49 | convolution fusion | flops 811663360 | bytes 5251080 | tf_op jit(solution)/shard_map/while/body/eval_jaxpr/cond/branch_1_fun/dot_general | solution.py:42
  303.0 6.0 %fusion.47 = f32[4096,64]{0,1:T(8,128)S(1)} fusion(f32[4096,64]{0,1:T(8,128)S(1)} %fusion.44, s32[]{:T(128)S(6)} %select_n.62, f32[1024,1024]{1,0:T(8,128)} %copy-done.1, f32[1024]{0:T(1024)S(1)} %get-tuple-element.383, f32[1024]{0:T(1024)S(1)} %get-tuple-element.382, f32[4096,64]{1,0:T(8,128)S(1)} %get-tuple-element.314, s32[]{:T(128)S(6)} %select_n.61, ...), kind=kOutput, calls=%fused_computation.52 | convolution fusion | flops 811728896 | bytes 5251084 | tf_op jit(solution)/shard_map/while/body/eval_jaxpr/cond/branch_1_fun/dot_general | solution.py:43
  309.0 1.1 fusion.77
  310.1 48.3 %all-reduce.5.cloned.1.call-done = (f32[2048,64]{0,1:T(8,128)}, f32[2048,64]{0,1:T(8,128)}) async-done(((f32[2048,64]{0,1:T(8,128)}, f32[2048,64]{0,1:T(8,128)}), (f32[2048,64]{0,1:T(8,128)}, f32[2048,64]{0,1:T(8,128)})) %all-reduce.5.cloned.1.call-update) | async-done | bytes 1048592 | tf_op jit(solution)/shard_map/psum | solution.py:102
  358.4 5.0 %collective-permute-start.4 = (f32[2048,64]{0,1:T(8,128)}, f32[2048,64]{0,1:T(8,128)S(1)}, u32[]{:S(2)}, u32[]{:S(2)}) collective-permute-start(f32[2048,64]{0,1:T(8,128)} %get-tuple-element.377), channel_id=1, source_target_pairs={{0,4},{4,8},{8,12},{12,16},{16,20},{20,24},{24,28},{28,32},{32,36}... | collective-permute-start | bytes 1572872 | tf_op jit(solution)/shard_map/ppermute | solution.py:15
  363.4 6.4 %collective-permute-done.4 = f32[2048,64]{0,1:T(8,128)S(1)} collective-permute-done((f32[2048,64]{0,1:T(8,128)}, f32[2048,64]{0,1:T(8,128)S(1)}, u32[]{:S(2)}, u32[]{:S(2)}) %collective-permute-start.4) | collective-permute-done | bytes 524320 | tf_op jit(solution)/shard_map/ppermute | solution.py:15
  369.8 1.1 add.182
  371.2 78.2 %psum.47 = f32[64,64]{0,1:T(8,128)S(1)} all-reduce(f32[64,64]{0,1:T(8,128)S(1)} %convolution_multiply_fusion), channel_id=1, replica_groups=mesh['rows'=64,'sub'=4] {'rows','sub'}, use_global_device_ids=true, to_apply=%region_16.19 | all-reduce | flops 4096 | bytes 32768 | tf_op jit(solution)/shard_map/psum | solution.py:107
  449.5 5.8 %cholesky.55 = f32[64,64]{1,0:T(8,128)S(1)} custom-call(f32[64,64]{1,0:T(8,128)S(1)} %fusion.67), custom_call_target="Cholesky" | custom-call | tf_op jit(solution)/shard_map/jit(cholesky)/cholesky | solution.py:108
  456.7 4.9 %custom-call.7 = f32[1,64,64]{1,2,0:T(8,128)S(1)} custom-call(f32[1,64,64]{2,1,0:T(8,128)S(1)} %fusion.65), custom_call_target="InvertDiagBlocksLowerTriangular" | custom-call | tf_op jit(solution)/shard_map/triangular_solve/custom-call.0 | solution.py:76
  461.6 1.4 convolution_bitcast_fusion
  (47 shorter events, 11.0 us)
Async XLA Ops:
  6.5 34.2 %copy-start.2 = (f32[2048,64]{0,1:T(8,128)S(1)}, f32[2048,64]{0,1:T(8,128)}, u32[]{:S(2)}) copy-start(f32[2048,64]{0,1:T(8,128)} %param.15) | copy-start | bytes 1572868
  6.5 141.4 %all-reduce.7.cloned.1.call-start = ((), (), s32[]{:S(2)}) async-start(), calls=%async_computation.1 | async-start | bytes 2097152 | tf_op jit(solution)/shard_map/psum | solution.py:102
  6.5 34.9 %collective-permute-start = (f32[2048,256]{1,0:T(8,128)}, f32[2048,256]{1,0:T(8,128)}, u32[]{:S(2)}, u32[]{:S(2)}) collective-permute-start(f32[2048,256]{1,0:T(8,128)} %param.14), channel_id=1, source_target_pairs={{4,0},{8,4},{12,8},{16,12},{20,16},{24,20},{28,24},{32,28},{36,32}... | collective-permute-start | bytes 6291464 | tf_op jit(solution)/shard_map/ppermute | solution.py:15
  11.8 28.9 %collective-permute-start.1 = (f32[2048,64]{0,1:T(8,128)}, f32[2048,64]{0,1:T(8,128)S(1)}, u32[]{:S(2)}, u32[]{:S(2)}) collective-permute-start(f32[2048,64]{0,1:T(8,128)} %param.15), channel_id=1, source_target_pairs={{4,0},{8,4},{12,8},{16,12},{20,16},{24,20},{28,24},{32,28},{36,32}... | collective-permute-start | bytes 1572872 | tf_op jit(solution)/shard_map/ppermute | solution.py:15
  55.8 2.0 copy-start
  78.9 2.0 copy-start
  94.5 263.9 %all-reduce.5.cloned.1.call-start = ((), (), s32[]{:S(2)}) async-start(), calls=%async_computation | async-start | bytes 2097152 | tf_op jit(solution)/shard_map/psum | solution.py:102
  147.9 11.4 %collective-permute-start.2 = (f32[2048,64]{0,1:T(8,128)}, f32[2048,64]{0,1:T(8,128)S(1)}, u32[]{:S(2)}, u32[]{:S(2)}) collective-permute-start(f32[2048,64]{0,1:T(8,128)} %get-tuple-element.379), channel_id=1, source_target_pairs={{0,4},{4,8},{8,12},{12,16},{16,20},{20,24},{24,28},{28,32},{32,36}... | collective-permute-start | bytes 1572872 | tf_op jit(solution)/shard_map/ppermute | solution.py:15
  251.7 10.5 %collective-permute-start.3 = (f32[2048,64]{0,1:T(8,128)S(1)}, f32[2048,64]{0,1:T(8,128)S(1)}, u32[]{:S(2)}, u32[]{:S(2)}) collective-permute-start(f32[2048,64]{0,1:T(8,128)S(1)} %convolution_bitcast_fusion.1), channel_id=1, source_target_pairs={{4,0},{8,4},{12,8},{16,12},{20,16},{24,20},{28,24},{32,28},{36,32}... | collective-permute-start | bytes 1572872 | tf_op jit(solution)/shard_map/ppermute | solution.py:15
  271.4 2.0 copy-start.1
  294.5 2.0 copy-start.1
  358.4 11.4 %collective-permute-start.4 = (f32[2048,64]{0,1:T(8,128)}, f32[2048,64]{0,1:T(8,128)S(1)}, u32[]{:S(2)}, u32[]{:S(2)}) collective-permute-start(f32[2048,64]{0,1:T(8,128)} %get-tuple-element.377), channel_id=1, source_target_pairs={{0,4},{4,8},{8,12},{12,16},{16,20},{20,24},{24,28},{28,32},{32,36}... | collective-permute-start | bytes 1572872 | tf_op jit(solution)/shard_map/ppermute | solution.py:15
Sparse Core Ops, SparseCore 0:
  94.7 53.1 all-reduce.6
  310.2 48.1 all-reduce.4
where the time goes:
time: 471 us; the launch traced here: 470 us
  blocking collectives  156 us (33%)
  waiting for transfers between devices  145 us (31%)
  matrix products  69 us (15%)
  other arithmetic  29.4 us (6%)
  local copies, waits for them, and re-layouts  23.6 us (5%)
  starting transfers between devices  20.1 us (4%)
  between operations  13.6 us (3%)
  loops' own time  13.2 us (3%)
    psum x2, blocking collectives, on_device(): gram = lax.psum(gram_part, ('rows', 'sub'))  156 us
    psum x2, waiting for transfers between devices, on_device(): own_sum, spill_sum = lax.psum((own_part, spill_part), 'sub')  102 us
    ppermute x5, waiting for transfers between devices, shifted(): return lax.ppermute(array, axis, pairs)  42.9 us
    dot_general x4, matrix products, work(): lax.dot_general(affinity, va, (((0,), (0,)), ((), ())), precision=highest...  24.1 us
    dot_general x4, matrix products, work(): lax.dot_general(xa, xb, (((1,), (1,)), ((), ())), precision=highest, pref...  21.3 us
    dot_general x4, matrix products, work(): jnp.dot(affinity, vb, precision=highest, preferred_element_type=jnp.float32)  21 us
    ppermute x5, starting transfers between devices, shifted(): return lax.ppermute(array, axis, pairs)  20 us
    another operation x6, other arithmetic, on_device(): lower = jnp.linalg.cholesky(gram)  13 us
  transfers between devices with their start and end apart: 7, of which 6 were waited for; matrix products, arithmetic and copies ran while one was open for 1% of the time, Pallas kernels for 0%

commit v1 on v0

--- a/solution.py
+++ b/solution.py
@@ -104,7 +104,7 @@
         whole = own_sum + incoming
         share = lax.dynamic_slice_in_dim(whole, member * quarter, quarter, 0)
         gram_part = gram_of(share, total_rows)
-        gram = lax.psum(gram_part, ("rows", "sub"))
+        gram = jnp.sum(lax.all_gather(gram_part, ("rows", "sub")), axis=0)
         lower = jnp.linalg.cholesky(gram)
         whole = right_solve(lower, whole)
         if step + 1 < ITERS:

time: 471 us -> 565 us (1.20)
  waiting for transfers between devices: 145 us -> 388 us
  blocking collectives: 156 us -> 0 us
  other arithmetic: 29.4 us -> 37.4 us
    all_gather x0 -> x2, waiting for transfers between devices: none -> 242 us  [on_device(): gram = jnp.sum(lax.all_gather(gram_part, ('rows', 'sub')), axis=0)]
    psum x2 -> x0, blocking collectives: 156 us -> none  [on_device(): gram = lax.psum(gram_part, ('rows', 'sub'))]
    reduce_sum x0 -> x2, other arithmetic: none -> 8.02 us  [on_device(): gram = jnp.sum(lax.all_gather(gram_part, ('rows', 'sub')), axis=0)]
  transfers between devices with their start and end apart: 7 -> 9, of which waited for: 6 -> 8; matrix products, arithmetic and copies ran while one was open for 1% -> 1% of each run, Pallas kernels for 0% -> 0%
where the time goes in v1:
time: 565 us; the launch traced here: 564 us
  waiting for transfers between devices  388 us (69%)
  matrix products  70.4 us (12%)
  other arithmetic  37.4 us (7%)
  local copies, waits for them, and re-layouts  23.4 us (4%)
  starting transfers between devices  19.8 us (4%)
  between operations  13.3 us (2%)
  loops' own time  12.1 us (2%)
    all_gather x2, waiting for transfers between devices, on_device(): gram = jnp.sum(lax.all_gather(gram_part, ('rows', 'sub')), axis=0)  242 us
    psum x2, waiting for transfers between devices, on_device(): own_sum, spill_sum = lax.psum((own_part, spill_part), 'sub')  102 us
    ppermute x5, waiting for transfers between devices, shifted(): return lax.ppermute(array, axis, pairs)  43.6 us
    dot_general x4, matrix products, work(): lax.dot_general(affinity, va, (((0,), (0,)), ((), ())), precision=highest...  24.1 us
    dot_general x4, matrix products, work(): lax.dot_general(xa, xb, (((1,), (1,)), ((), ())), precision=highest, pref...  21.4 us
    dot_general x4, matrix products, work(): jnp.dot(affinity, vb, precision=highest, preferred_element_type=jnp.float32)  21 us
    ppermute x5, starting transfers between devices, shifted(): return lax.ppermute(array, axis, pairs)  19.3 us
    another operation x6, other arithmetic, on_device(): lower = jnp.linalg.cholesky(gram)  13 us
  transfers between devices with their start and end apart: 9, of which 8 were waited for; matrix products, arithmetic and copies ran while one was open for 1% of the time, Pallas kernels for 0%

profile of v1, /device:TPU:1, one launch (start us, length us, event | category | flops | bytes accessed | tf_op | source)
XLA Modules:
  0.0 564.3 jit_solution(3919607919161031135)
XLA Ops:
  6.5 5.3 collective-permute-start
  11.8 1.9 collective-permute-start.1
  15.2 3.1 constant_dynamic-update-slice_fusion.1
  18.3 22.5 %collective-permute-done.1 = f32[2048,64]{0,1:T(8,128)S(1)} collective-permute-done((f32[2048,64]{0,1:T(8,128)}, f32[2048,64]{0,1:T(8,128)S(1)}, u32[]{:S(2)}, u32[]{:S(2)}) %collective-permute-start.1) | collective-permute-done | bytes 524320 | tf_op jit(solution)/shard_map/ppermute | solution.py:15
  41.4 3.1 constant_dynamic-update-slice_fusion
  44.5 2.8 multiply_reduce_fusion
  47.3 45.5 %while.32 = (s32[]{:T(128)}, f32[4096,64]{0,1:T(8,128)S(1)}, s32[2,2]{1,0:T(2,128)S(1)}, s32[]{:T(128)}, f32[4096]{0:T(1024)S(1)}, /*index=5*/f32[4096,256]{1,0:...) while((s32[]{:T(128)}, f32[4096,64]{0,1:T(8,128)S(1)}, s32[2,2]{1,0:T(2,128)S(1)}, s32[]{:T(128)}, ...), condition=%wide.region_4.5_spmd, body=%wide.region_1.0_spmd.sunk | while | flops 4844617728 | bytes 33587592 | solution.py:59
  48.5 21.6 %conditional.4 = (f32[4096,64]{0,1:T(8,128)S(1)}) conditional(s32[]{:T(128)} %convert_element_type.22, f32[4096,64]{0,1:T(8,128)S(1)} %get-tuple-element.484, (s32[]{:T(128)}, s32[]{:T(128)}, f32[4096,64]{0,1:T(8,128)S(1)}, f32[4096]{0:T(1024)S(1)}, s32[2,2]{1,0:T(2,128)S(1)}, /*index=5*/s32[]{:T(128)}, f32[4096,256]{1,0:T(8,128)}, ...), branch_computations={%region_2.2_spmd, %region_3.3_spmd} | conditional | flops 4844617728 | bytes 33587412 | solution.py:56
  50.3 5.4 fusion.17
  55.7 1.9 copy-done
  57.7 5.3 fusion.13
  64.1 6.0 %fusion.16 = f32[4096,64]{0,1:T(8,128)S(1)} fusion(f32[4096,64]{0,1:T(8,128)S(1)} %fusion.13, s32[]{:T(128)S(6)} %select_n.59, f32[1024,1024]{1,0:T(8,128)} %copy-done, f32[1024]{0:T(1024)S(1)} %get-tuple-element.381, f32[1024]{0:T(1024)S(1)} %get-tuple-element.380, f32[4096,64]{1,0:T(8,128)S(1)} %get-tuple-element.298, s32[]{:T(128)S(6)} %select_n.58, ...), kind=kOutput, calls=%fused_computation.18 | convolution fusion | flops 811728896 | bytes 5251084 | tf_op jit(solution)/shard_map/while/body/eval_jaxpr/cond/branch_1_fun/dot_general | solution.py:43
  71.3 21.5 %conditional.4 = (f32[4096,64]{0,1:T(8,128)S(1)}) conditional(s32[]{:T(128)} %convert_element_type.22, f32[4096,64]{0,1:T(8,128)S(1)} %get-tuple-element.484, (s32[]{:T(128)}, s32[]{:T(128)}, f32[4096,64]{0,1:T(8,128)S(1)}, f32[4096]{0:T(1024)S(1)}, s32[2,2]{1,0:T(2,128)S(1)}, /*index=5*/s32[]{:T(128)}, f32[4096,256]{1,0:T(8,128)}, ...), branch_computations={%region_2.2_spmd, %region_3.3_spmd} | conditional | flops 4844617728 | bytes 33587412 | solution.py:56
  73.1 5.3 fusion.17
  78.5 1.9 copy-done
  80.4 5.3 fusion.13
  86.8 6.0 %fusion.16 = f32[4096,64]{0,1:T(8,128)S(1)} fusion(f32[4096,64]{0,1:T(8,128)S(1)} %fusion.13, s32[]{:T(128)S(6)} %select_n.59, f32[1024,1024]{1,0:T(8,128)} %copy-done, f32[1024]{0:T(1024)S(1)} %get-tuple-element.381, f32[1024]{0:T(1024)S(1)} %get-tuple-element.380, f32[4096,64]{1,0:T(8,128)S(1)} %get-tuple-element.298, s32[]{:T(128)S(6)} %select_n.58, ...), kind=kOutput, calls=%fused_computation.18 | convolution fusion | flops 811728896 | bytes 5251084 | tf_op jit(solution)/shard_map/while/body/eval_jaxpr/cond/branch_1_fun/dot_general | solution.py:43
  92.9 1.1 fusion.78
  94.0 53.1 %all-reduce.7.cloned.1.call-done = (f32[2048,64]{0,1:T(8,128)}, f32[2048,64]{0,1:T(8,128)}) async-done(((f32[2048,64]{0,1:T(8,128)}, f32[2048,64]{0,1:T(8,128)}), (f32[2048,64]{0,1:T(8,128)}, f32[2048,64]{0,1:T(8,128)})) %all-reduce.7.cloned.1.call-update) | async-done | bytes 1048592 | tf_op jit(solution)/shard_map/psum | solution.py:102
  147.1 5.0 collective-permute-start.2
  152.1 6.4 %collective-permute-done.2 = f32[2048,64]{0,1:T(8,128)S(1)} collective-permute-done((f32[2048,64]{0,1:T(8,128)}, f32[2048,64]{0,1:T(8,128)S(1)}, u32[]{:S(2)}, u32[]{:S(2)}) %collective-permute-start.2) | collective-permute-done | bytes 524320 | tf_op jit(solution)/shard_map/ppermute | solution.py:15
  158.5 1.1 add.176
  160.7 121.0 %all-gather.5.cloned.1.call-done = f32[16384,64]{1,0:T(8,128)} async-done(((f32[64,64]{1,0:T(8,128)}), f32[16384,64]{1,0:T(8,128)}) %all-gather.5.cloned.1.call-update) | async-done | bytes 4194320 | tf_op jit(solution)/shard_map/all_gather | solution.py:107
  281.7 4.0 reduce_sum.28
  285.9 5.8 %cholesky.44 = f32[64,64]{1,0:T(8,128)S(1)} custom-call(f32[64,64]{1,0:T(8,128)S(1)} %fusion.69), custom_call_target="Cholesky" | custom-call | tf_op jit(solution)/shard_map/jit(cholesky)/cholesky | solution.py:108
  293.0 4.9 custom-call.6
  298.6 2.2 collective-permute-start.3
  300.7 8.3 %collective-permute-done.3 = f32[2048,64]{0,1:T(8,128)S(1)} collective-permute-done((f32[2048,64]{0,1:T(8,128)S(1)}, f32[2048,64]{0,1:T(8,128)S(1)}, u32[]{:S(2)}, u32[]{:S(2)}) %collective-permute-start.3) | collective-permute-done | bytes 524320 | tf_op jit(solution)/shard_map/ppermute | solution.py:15
  309.8 45.5 %while.33 = (s32[]{:T(128)}, f32[4096,64]{0,1:T(8,128)S(1)}, s32[2,2]{1,0:T(2,128)S(1)}, s32[]{:T(128)}, f32[4096]{0:T(1024)S(1)}, /*index=5*/f32[4096,256]{1,0:...) while((s32[]{:T(128)}, f32[4096,64]{0,1:T(8,128)S(1)}, s32[2,2]{1,0:T(2,128)S(1)}, s32[]{:T(128)}, ...), condition=%wide.region_13.16_spmd, body=%wide.region_10.15_spmd.sunk | while | flops 4844617728 | bytes 33587592 | solution.py:59
  311.0 21.6 %conditional.5 = (f32[4096,64]{0,1:T(8,128)S(1)}) conditional(s32[]{:T(128)} %convert_element_type.23, f32[4096,64]{0,1:T(8,128)S(1)} %get-tuple-element.511, (s32[]{:T(128)}, s32[]{:T(128)}, f32[4096,64]{0,1:T(8,128)S(1)}, f32[4096]{0:T(1024)S(1)}, s32[2,2]{1,0:T(2,128)S(1)}, /*index=5*/s32[]{:T(128)}, f32[4096,256]{1,0:T(8,128)}, ...), branch_computations={%region_11.13_spmd, %region_12.14_spmd} | conditional | flops 4844617728 | bytes 33587412 | solution.py:56
  312.8 5.4 fusion.48
  318.2 1.9 copy-done.1
  320.2 5.3 fusion.44
  326.6 6.0 %fusion.47 = f32[4096,64]{0,1:T(8,128)S(1)} fusion(f32[4096,64]{0,1:T(8,128)S(1)} %fusion.44, s32[]{:T(128)S(6)} %select_n.62, f32[1024,1024]{1,0:T(8,128)} %copy-done.1, f32[1024]{0:T(1024)S(1)} %get-tuple-element.383, f32[1024]{0:T(1024)S(1)} %get-tuple-element.382, f32[4096,64]{1,0:T(8,128)S(1)} %get-tuple-element.314, s32[]{:T(128)S(6)} %select_n.61, ...), kind=kOutput, calls=%fused_computation.52 | convolution fusion | flops 811728896 | bytes 5251084 | tf_op jit(solution)/shard_map/while/body/eval_jaxpr/cond/branch_1_fun/dot_general | solution.py:43
  333.8 21.5 %conditional.5 = (f32[4096,64]{0,1:T(8,128)S(1)}) conditional(s32[]{:T(128)} %convert_element_type.23, f32[4096,64]{0,1:T(8,128)S(1)} %get-tuple-element.511, (s32[]{:T(128)}, s32[]{:T(128)}, f32[4096,64]{0,1:T(8,128)S(1)}, f32[4096]{0:T(1024)S(1)}, s32[2,2]{1,0:T(2,128)S(1)}, /*index=5*/s32[]{:T(128)}, f32[4096,256]{1,0:T(8,128)}, ...), branch_computations={%region_11.13_spmd, %region_12.14_spmd} | conditional | flops 4844617728 | bytes 33587412 | solution.py:56
  335.6 5.3 fusion.48
  340.9 1.9 copy-done.1
  342.9 5.3 fusion.44
  349.3 6.0 %fusion.47 = f32[4096,64]{0,1:T(8,128)S(1)} fusion(f32[4096,64]{0,1:T(8,128)S(1)} %fusion.44, s32[]{:T(128)S(6)} %select_n.62, f32[1024,1024]{1,0:T(8,128)} %copy-done.1, f32[1024]{0:T(1024)S(1)} %get-tuple-element.383, f32[1024]{0:T(1024)S(1)} %get-tuple-element.382, f32[4096,64]{1,0:T(8,128)S(1)} %get-tuple-element.314, s32[]{:T(128)S(6)} %select_n.61, ...), kind=kOutput, calls=%fused_computation.52 | convolution fusion | flops 811728896 | bytes 5251084 | tf_op jit(solution)/shard_map/while/body/eval_jaxpr/cond/branch_1_fun/dot_general | solution.py:43
  356.7 48.7 %all-reduce.5.cloned.1.call-done = (f32[2048,64]{0,1:T(8,128)}, f32[2048,64]{0,1:T(8,128)}) async-done(((f32[2048,64]{0,1:T(8,128)}, f32[2048,64]{0,1:T(8,128)}), (f32[2048,64]{0,1:T(8,128)}, f32[2048,64]{0,1:T(8,128)})) %all-reduce.5.cloned.1.call-update) | async-done | bytes 1048592 | tf_op jit(solution)/shard_map/psum | solution.py:102
  405.4 5.0 collective-permute-start.4
  410.4 6.4 %collective-permute-done.4 = f32[2048,64]{0,1:T(8,128)S(1)} collective-permute-done((f32[2048,64]{0,1:T(8,128)}, f32[2048,64]{0,1:T(8,128)S(1)}, u32[]{:S(2)}, u32[]{:S(2)}) %collective-permute-start.4) | collective-permute-done | bytes 524320 | tf_op jit(solution)/shard_map/ppermute | solution.py:15
  416.8 1.1 add.178
  418.9 121.2 %all-gather.7.cloned.1.call-done = f32[16384,64]{1,0:T(8,128)} async-done(((f32[64,64]{1,0:T(8,128)}), f32[16384,64]{1,0:T(8,128)}) %all-gather.7.cloned.1.call-update) | async-done | bytes 4194320 | tf_op jit(solution)/shard_map/all_gather | solution.py:107
  540.1 4.0 reduce_sum.29
  544.2 5.8 %cholesky.55 = f32[64,64]{1,0:T(8,128)S(1)} custom-call(f32[64,64]{1,0:T(8,128)S(1)} %fusion.67), custom_call_target="Cholesky" | custom-call | tf_op jit(solution)/shard_map/jit(cholesky)/cholesky | solution.py:108
  551.4 4.9 custom-call.7
  556.3 1.4 convolution_bitcast_fusion
  (53 shorter events, 14.3 us)
Async XLA Ops:
  6.5 34.2 %copy-start.2 = (f32[2048,64]{0,1:T(8,128)S(1)}, f32[2048,64]{0,1:T(8,128)}, u32[]{:S(2)}) copy-start(f32[2048,64]{0,1:T(8,128)} %param.15) | copy-start | bytes 1572868
  6.5 140.6 %all-reduce.7.cloned.1.call-start = ((), (), s32[]{:S(2)}) async-start(), calls=%async_computation.3 | async-start | bytes 2097152 | tf_op jit(solution)/shard_map/psum | solution.py:102
  6.5 34.9 %collective-permute-start = (f32[2048,256]{1,0:T(8,128)}, f32[2048,256]{1,0:T(8,128)}, u32[]{:S(2)}, u32[]{:S(2)}) collective-permute-start(f32[2048,256]{1,0:T(8,128)} %param.14), channel_id=1, source_target_pairs={{4,0},{8,4},{12,8},{16,12},{20,16},{24,20},{28,24},{32,28},{36,32}... | collective-permute-start | bytes 6291464 | tf_op jit(solution)/shard_map/ppermute | solution.py:15
  11.8 28.9 %collective-permute-start.1 = (f32[2048,64]{0,1:T(8,128)}, f32[2048,64]{0,1:T(8,128)S(1)}, u32[]{:S(2)}, u32[]{:S(2)}) collective-permute-start(f32[2048,64]{0,1:T(8,128)} %param.15), channel_id=1, source_target_pairs={{4,0},{8,4},{12,8},{16,12},{20,16},{24,20},{28,24},{32,28},{36,32}... | collective-permute-start | bytes 1572872 | tf_op jit(solution)/shard_map/ppermute | solution.py:15
  55.7 1.9 copy-start
  78.4 1.9 copy-start
  94.0 187.8 %all-gather.5.cloned.1.call-start = ((), (), s32[]{:S(2)}) async-start(), calls=%async_computation | async-start | bytes 8421376 | tf_op jit(solution)/shard_map/all_gather | solution.py:107
  147.1 11.4 %collective-permute-start.2 = (f32[2048,64]{0,1:T(8,128)}, f32[2048,64]{0,1:T(8,128)S(1)}, u32[]{:S(2)}, u32[]{:S(2)}) collective-permute-start(f32[2048,64]{0,1:T(8,128)} %get-tuple-element.379), channel_id=1, source_target_pairs={{0,4},{4,8},{8,12},{12,16},{16,20},{20,24},{24,28},{28,32},{32,36}... | collective-permute-start | bytes 1572872 | tf_op jit(solution)/shard_map/ppermute | solution.py:15
  160.5 244.9 %all-reduce.5.cloned.1.call-start = ((), (), s32[]{:S(2)}) async-start(), calls=%async_computation.2 | async-start | bytes 2097152 | tf_op jit(solution)/shard_map/psum | solution.py:102
  298.6 10.5 %collective-permute-start.3 = (f32[2048,64]{0,1:T(8,128)S(1)}, f32[2048,64]{0,1:T(8,128)S(1)}, u32[]{:S(2)}, u32[]{:S(2)}) collective-permute-start(f32[2048,64]{0,1:T(8,128)S(1)} %convolution_bitcast_fusion.1), channel_id=1, source_target_pairs={{4,0},{8,4},{12,8},{16,12},{20,16},{24,20},{28,24},{32,28},{36,32}... | collective-permute-start | bytes 1572872 | tf_op jit(solution)/shard_map/ppermute | solution.py:15
  318.2 1.9 copy-start.1
  340.9 1.9 copy-start.1
  356.4 183.7 %all-gather.7.cloned.1.call-start = ((), (), s32[]{:S(2)}) async-start(), calls=%async_computation.1 | async-start | bytes 8421376 | tf_op jit(solution)/shard_map/all_gather | solution.py:107
  405.4 11.4 %collective-permute-start.4 = (f32[2048,64]{0,1:T(8,128)}, f32[2048,64]{0,1:T(8,128)S(1)}, u32[]{:S(2)}, u32[]{:S(2)}) collective-permute-start(f32[2048,64]{0,1:T(8,128)} %get-tuple-element.377), channel_id=1, source_target_pairs={{0,4},{4,8},{8,12},{12,16},{16,20},{20,24},{24,28},{28,32},{32,36}... | collective-permute-start | bytes 1572872 | tf_op jit(solution)/shard_map/ppermute | solution.py:15
Sparse Core Ops, SparseCore 0:
  94.1 52.9 all-reduce.6
  160.6 121.0 all-gather.4
  356.6 48.8 all-reduce.4
  419.0 121.0 all-gather.6
